TPU v7x, 512 devices: a whole 4x8x8 slice. The times are simulated.
512 devices in a mesh: seq: 64 (over z, y), head: 8 (over x, core).
Axes of the slice: x: 4, y: 8, z: 8, core: 2. Of those that a mesh axis runs over, the one named last changes fastest.
Arguments:
- raw_keys: bfloat16 [2, 65536, 8, 128], P(None, 'seq', 'head'), may hold values from -6 to 6
- raw_values: bfloat16 [2, 65536, 8, 128], P(None, 'seq', 'head'), may hold values from -6 to 6
- phase: int32 [2], replicated, may hold values from 0 to 255, as said below
- ratio: int32 [2, 64], replicated, may hold values from 8 to 32, as said below
- resident_len: int32 [2, 64], replicated, may hold values from 1 to 256, as said below
- beacon_queries: bfloat16 [2, 8192, 8, 8, 128], P(None, 'seq', 'head'), may hold values from -150 to 150
- beacon_wk: bfloat16 [8192, 1024], P('seq', 'head'), may hold values from -0.125 to 0.125
- beacon_wv: bfloat16 [8192, 1024], P('seq', 'head'), may hold values from -0.125 to 0.125
- resident_keys: bfloat16 [2, 16384, 8, 128], P(None, 'seq', 'head'), may hold values from -6 to 6
- resident_values: bfloat16 [2, 16384, 8, 128], P(None, 'seq', 'head'), may hold values from -6 to 6
- decode_queries: bfloat16 [4, 2, 8, 8, 128], P(None, None, 'head'), may hold values from -150 to 150
- out_weight: bfloat16 [8192, 8192], P('head', 'seq'), may hold values from -0.0625 to 0.0625
Outputs:
- beacon_keys: bfloat16 [2, 8192, 8, 128], P(None, 'seq', 'head')
- beacon_values: bfloat16 [2, 8192, 8, 128], P(None, 'seq', 'head')
- projected: bfloat16 [4, 2, 8192], P(None, None, 'seq')
Inputs may be any that keep to these rules, and one draw needn't show every extreme that they name: `phase`: some request has 255. `ratio`: each value is 1024 // 128 times 1, 2 or 4; both ends occur. `resident_len`: some pair has 256.
All inputs are finite; a program needn't handle non-finite values.
Results may differ from a plain program's by a relative error of at most 0.025.
Values may be sent and summed in bfloat16 or wider, within the bound.
No kernel may reach another device: no remote copies, remote signals or barrier semaphores. Data moves between devices by JAX's collectives and lax.ppermute only.
A program may use at most 64 MiB of HBM per device.

v0:
```python
import math
import jax
import jax.numpy as jnp
from jax import lax
from jax.sharding import PartitionSpec as P

G = 8
INTERVAL = 1024
NB = 128
OFF = 256
STEPS = 4
masked_score = -1e30


def shifted(value, axis, steps):
    count = lax.axis_size(axis)
    first, last = (max(0, -steps), min(count, count - steps))
    return lax.ppermute(value, axis, [(source, source + steps) for source in range(first, last)])


def pool_part(queries, key_rows, value_rows, positions, present, reaches):
    inv_root = 1.0 / math.sqrt(queries.shape[-1])

    def per_request(members):
        query_block, key_block, value_block, position_row, present_row, reach_row = members
        scores = (
            jnp.einsum("jkgd,ikd->jkgi", query_block, key_block, preferred_element_type=jnp.float32)
            * inv_root
        )
        allowed = (
            present_row[None, :]
            & (position_row[None, :] >= 0)
            & (position_row[None, :] < INTERVAL)
            & (position_row[None, :] < reach_row[:, None])
        )
        cache_mask = allowed[:, None, None, :]
        row_peak = jnp.max(jnp.where(cache_mask, scores, masked_score), axis=-1)
        weights = jnp.where(cache_mask, jnp.exp(scores - row_peak[..., None]), 0.0)
        weight_sum = jnp.sum(weights, axis=-1)
        weighted = jnp.einsum(
            "jkgi,ikd->jkgd",
            weights.astype(jnp.bfloat16),
            value_block,
            preferred_element_type=jnp.float32,
        )
        return (row_peak, weight_sum, weighted)

    return lax.map(per_request, (queries, key_rows, value_rows, positions, present, reaches))


def body(
    raw_keys,
    raw_values,
    phase,
    ratio,
    resident_len,
    beacon_queries,
    beacon_wk,
    beacon_wv,
    resident_keys,
    resident_values,
    decode_queries,
    out_weight,
):
    requests = raw_keys.shape[0]
    kv_local = raw_keys.shape[2]
    head_dim = raw_keys.shape[3]
    shard_index = lax.axis_index("seq")
    shard_count = lax.axis_size("seq")
    is_first = shard_index == 0
    is_last = shard_index == shard_count - 1
    own_ratio = lax.dynamic_index_in_dim(ratio, shard_index, 1, keepdims=False)
    slot_ids = jnp.arange(NB, dtype=jnp.int32)
    lead_in = jnp.where(is_first, phase, 0)
    reaches = (slot_ids[None, :] + 1) * own_ratio[:, None] + lead_in[:, None]
    tail_keys = raw_keys[:, INTERVAL - OFF :]
    tail_values = raw_values[:, INTERVAL - OFF :]
    own_positions = jnp.arange(INTERVAL, dtype=jnp.int32)[None, :] + phase[:, None]
    rim_ids = jnp.arange(OFF, dtype=jnp.int32)
    rim_positions = rim_ids[None, :] - OFF + phase[:, None]
    near_keys, near_values = shifted((tail_keys, tail_values), "seq", 1)
    key_rows = jnp.concatenate([near_keys, raw_keys], axis=1)
    value_rows = jnp.concatenate([near_values, raw_values], axis=1)
    positions = jnp.concatenate([rim_positions, own_positions], axis=1)
    present = jnp.logical_not(is_first) | (positions >= phase[:, None])
    pooled_parts = pool_part(beacon_queries, key_rows, value_rows, positions, present, reaches)
    pooled = (pooled_parts[2] / pooled_parts[1][..., None]).astype(jnp.bfloat16)
    pooled_flat = pooled.reshape(requests * NB, kv_local * G * head_dim)
    pooled_whole = lax.all_gather(pooled_flat, "head", axis=1, tiled=True)
    key_sum = jnp.dot(
        pooled_whole,
        lax.all_gather(beacon_wk, "seq", axis=0, tiled=True),
        preferred_element_type=jnp.float32,
    )
    value_sum = jnp.dot(
        pooled_whole,
        lax.all_gather(beacon_wv, "seq", axis=0, tiled=True),
        preferred_element_type=jnp.float32,
    )
    made_keys = key_sum
    made_values = value_sum
    made_keys = made_keys.reshape(requests, NB, kv_local, head_dim)
    made_values = made_values.reshape(requests, NB, kv_local, head_dim)
    slot_live = slot_ids[None, :] < (INTERVAL // own_ratio)[:, None]
    beacon_keys = jnp.where(slot_live[:, :, None, None], made_keys, 0.0).astype(jnp.bfloat16)
    beacon_values = jnp.where(slot_live[:, :, None, None], made_values, 0.0).astype(jnp.bfloat16)
    cache_keys = jnp.concatenate([resident_keys, beacon_keys, tail_keys], axis=1)
    cache_values = jnp.concatenate([resident_values, beacon_values, tail_values], axis=1)
    own_len = lax.dynamic_index_in_dim(resident_len, shard_index, 1, keepdims=False)
    resident_ok = jnp.arange(resident_keys.shape[1], dtype=jnp.int32)[None, :] < own_len[:, None]
    leftover_ok = (rim_ids[None, :] >= OFF - phase[:, None]) & is_last
    usable = jnp.concatenate([resident_ok, slot_live, leftover_ok], axis=1)
    inv_root = 1.0 / math.sqrt(head_dim)
    scores = (
        jnp.einsum(
            "srkgd,rikd->rksgi", decode_queries, cache_keys, preferred_element_type=jnp.float32
        )
        * inv_root
    )
    cache_mask = usable[:, None, None, None, :]
    row_peak = jnp.max(jnp.where(cache_mask, scores, masked_score), axis=-1)
    weights = jnp.where(cache_mask, jnp.exp(scores - row_peak[..., None]), 0.0)
    weight_sum = jnp.sum(weights, axis=-1)
    weighted = jnp.einsum(
        "rksgi,rikd->rksgd",
        weights.astype(jnp.bfloat16),
        cache_values,
        preferred_element_type=jnp.float32,
    )
    global_peak = lax.pmax(row_peak, "seq")
    rescale = jnp.exp(row_peak - global_peak)
    total_sum, total_weighted = lax.psum(
        (weight_sum * rescale, weighted * rescale[..., None]), "seq"
    )
    attended = (total_weighted / total_sum[..., None]).astype(jnp.bfloat16)
    attended = jnp.transpose(attended, (2, 0, 1, 3, 4)).reshape(
        STEPS * requests, kv_local * G * head_dim
    )
    partial_value = jnp.dot(attended, out_weight, preferred_element_type=jnp.float32)
    summed = lax.psum(partial_value, "head")
    projected = summed.astype(jnp.bfloat16).reshape(STEPS, requests, out_weight.shape[1])
    return (beacon_keys, beacon_values, projected)


def solution(mesh):
    return jax.shard_map(
        body,
        mesh=mesh,
        in_specs=(
            P(None, "seq", "head", None),
            P(None, "seq", "head", None),
            P(),
            P(),
            P(),
            P(None, "seq", "head", None, None),
            P("seq", "head"),
            P("seq", "head"),
            P(None, "seq", "head", None),
            P(None, "seq", "head", None),
            P(None, None, "head", None, None),
            P("head", "seq"),
        ),
        out_specs=(
            P(None, "seq", "head", None),
            P(None, "seq", "head", None),
            P(None, None, "seq"),
        ),
        check_vma=False,
    )
```

profile of v0, /device:TPU:1, one launch (start us, length us, event | category | flops | bytes accessed | tf_op | source)
XLA Modules:
  0.0 666.6 jit_solution(5328392180371530264)
XLA Ops:
  7.2 0.0 copy-start
  7.2 0.0 copy-start.1
  7.2 0.0 all-gather.6.cloned.1.call-start
  7.2 1.0 slice.9
  8.2 4.7 collective-permute-start.1
  12.9 0.9 slice.8
  13.8 2.6 collective-permute-start
  16.4 0.0 all-gather.6.cloned.1.call-update
  16.4 0.0 all-gather.4.cloned.1.call-start
  16.5 0.7 broadcast_subtract_fusion
  17.2 0.7 iota_add_fusion
  17.9 1.2 copy.32
  19.2 0.7 broadcast_add_fusion
  19.9 0.7 compare_or_fusion
  20.6 1.0 fusion.44
  21.7 0.1 multiply_add_fusion
  21.8 0.0 collective-permute-done
  21.8 1.1 pad_maximum_fusion
  22.9 0.0 collective-permute-done.1
  22.9 1.0 copy.31
  23.9 0.9 pad_maximum_fusion.1
  24.8 0.0 copy-done.1
  24.8 8.6 %while.12 = (s32[]{:T(128)}, f32[2,128,1,8]{1,3,2,0:T(8,128)S(1)}, f32[2,128,1,8,128]{1,4,3,2,0:T(8,128)S(1)}, pred[2,1280]{1,0:T(4,128)(4,1)S(1)}, s32[2,1280]{...) while((s32[]{:T(128)}, f32[2,128,1,8]{1,3,2,0:T(8,128)S(1)}, ...), condition=%wide.region_3.4_spmd, body=%wide.region_0.3_spmd.sunk | while | flops 685837312 | bytes 21023128 | solution.py:48
  24.9 0.9 compare_and_fusion.3
  25.8 0.9 fusion.65
  26.8 0.0 copy-done.2
  26.8 1.2 fusion.67
  27.9 1.1 fusion.66
  29.1 0.0 copy-start.2
  29.2 0.9 compare_and_fusion.3
  30.2 0.9 fusion.65
  31.1 0.0 copy-done.2
  31.1 1.2 fusion.67
  32.3 1.1 fusion.66
  33.4 0.1 divide_convert_fusion
  33.5 0.3 copy.34
  33.8 0.9 copy.60
  34.8 0.0 all-gather.4.cloned.1.call-update
  34.8 0.0 all-gather.8.cloned.1.call-start
  34.8 0.7 all-gather.8.cloned.1.call-update
  35.5 0.1 iota_compare_fusion.1
  35.6 0.1 iota_compare_fusion
  35.7 0.1 compare_and_fusion.1
  35.8 64.2 %all-gather.6.cloned.1.call-done = bf16[8192,128]{1,0:T(8,128)(2,1)} async-done(((bf16[128,128]{1,0:T(8,128)(2,1)}), bf16[8192,128]{1,0:T(8,128)(2,1)}) %all-gather.6.cloned.1.call-update) | async-done | bytes 2097168 | tf_op jit(solution)/shard_map/all_gather | solution.py:92
  99.9 40.7 %all-gather.4.cloned.1.call-done = bf16[256,8192]{1,0:T(8,128)(2,1)} async-done(((bf16[256,1024]{1,0:T(8,128)(2,1)}), bf16[256,8192]{1,0:T(8,128)(2,1)}) %all-gather.4.cloned.1.call-update) | async-done | bytes 4194320 | tf_op jit(solution)/shard_map/all_gather | solution.py:89
  140.6 4.1 fusion.48
  144.7 0.0 copy-start.5
  144.8 0.0 copy-start.7
  144.8 0.0 copy-start.6
  144.8 78.4 %all-gather.8.cloned.1.call-done = bf16[8192,128]{1,0:T(8,128)(2,1)} async-done(((bf16[128,128]{1,0:T(8,128)(2,1)}), bf16[8192,128]{1,0:T(8,128)(2,1)}) %all-gather.8.cloned.1.call-update) | async-done | bytes 2097168 | tf_op jit(solution)/shard_map/all_gather | solution.py:97
  223.1 4.1 fusion.49
  227.2 0.1 select_convert_fusion
  227.4 0.0 copy-start.3
  227.4 0.0 copy-start.4
  227.4 0.0 copy-done.5
  227.4 0.3 select_reduce_fusion
  227.7 0.2 bitcast_reduce_fusion
  227.9 113.3 %pmax.7 = f32[2,1,4,8]{3,2,0,1:T(4,128)S(1)} all-reduce(f32[2,1,4,8]{3,2,0,1:T(4,128)S(1)} %bitcast.153), channel_id=1, replica_groups=mesh['seq'=64,'head'=8] {'seq'}, use_global_device_ids=true, to_apply=%region_5.6 | all-reduce | flops 64 | bytes 512 | tf_op jit(solution)/shard_map/pmax | solution.py:130
  341.3 0.2 fusion.25
  341.5 219.7 %all-reduce = (f32[2,1,4,8,128]{4,3,2,0,1:T(8,128)S(1)}, f32[2,4,8]{2,1,0:T(4,128)S(1)}) all-reduce(f32[2,1,4,8,128]{4,3,2,0,1:T(8,128)S(1)} %fusion.25, f32[2,4,8]{2,1,0:T(4,128)S(1)} %get-tuple-element.101), channel_id=1, replica_groups=mesh['seq'=64,'head'=8] {'seq'}, use_global_device_ids=true, to_apply=%region_6.7 | all-reduce | flops 8256 | bytes 66048 | tf_op jit(solution)/shard_map/psum | solution.py:132
  561.2 0.1 fusion.41
  561.3 0.0 copy-done
  561.3 0.1 fusion.37
  561.5 98.6 %psum.23 = bf16[8,128]{1,0:T(8,128)(2,1)} all-reduce(f32[8,128]{1,0:T(8,128)S(1)} %fusion.37), channel_id=1, replica_groups=mesh['seq'=64,'head'=8] {'head'}, use_global_device_ids=true, to_apply=%region_9.10 | all-reduce | flops 1024 | bytes 6144 | tf_op jit(solution)/shard_map/psum | solution.py:140
  (23 shorter events, 0.3 us)
Async XLA Ops:
  7.2 554.2 %copy-start = (bf16[1024,128]{1,0:T(8,128)(2,1)S(1)}, bf16[1024,128]{1,0:T(8,128)(2,1)}, u32[]{:S(2)}) copy-start(bf16[1024,128]{1,0:T(8,128)(2,1)} %param.25) | copy-start | bytes 786436
  7.2 17.6 %copy-start.1 = (bf16[2,128,1,8,128]{4,3,2,1,0:T(8,128)(2,1)S(1)}, bf16[2,128,1,8,128]{4,3,2,1,0:T(8,128)(2,1)}, u32[]{:S(2)}) copy-start(bf16[2,128,1,8,128]{4,3,2,1,0:T(8,128)(2,1)} %param.19) | copy-start | bytes 1572868
  7.2 92.7 %all-gather.6.cloned.1.call-start = ((), (), s32[]{:S(2)}) async-start(), calls=%async_computation.1 | async-start | bytes 2129920 | tf_op jit(solution)/shard_map/all_gather | solution.py:92
  8.2 14.6 %collective-permute-start.1 = (bf16[2,256,1,128]{3,1,0,2:T(8,128)(2,1)S(1)}, bf16[2,256,1,128]{3,1,0,2:T(8,128)(2,1)}, u32[]{:S(2)}, u32[]{:S(2)}) collective-permute-start(bf16[2,256,1,128]{3,1,0,2:T(8,128)(2,1)S(1)} %slice.9), channel_id=1, source_target_pairs={{0,8},{8,16},{16,24},{24,32},{32,40},{40,48},{48,56},{56,64},{64,7... | collective-permute-start | bytes 393224 | tf_op jit(solution)/shard_map/ppermute | solution.py:18
  13.8 7.9 %collective-permute-start = (bf16[2,256,1,128]{3,1,0,2:T(8,128)(2,1)S(1)}, bf16[2,256,1,128]{3,1,0,2:T(8,128)(2,1)S(1)}, u32[]{:S(2)}, u32[]{:S(2)}) collective-permute-start(bf16[2,256,1,128]{3,1,0,2:T(8,128)(2,1)S(1)} %slice.8), channel_id=1, source_target_pairs={{0,8},{8,16},{16,24},{24,32},{32,40},{40,48},{48,56},{56,64},{64,7... | collective-permute-start | bytes 393224 | tf_op jit(solution)/shard_map/ppermute | solution.py:18
  16.4 124.2 %all-gather.4.cloned.1.call-start = ((), (), s32[]{:S(2)}) async-start(), calls=%async_computation | async-start | bytes 4718592 | tf_op jit(solution)/shard_map/all_gather | solution.py:89
  24.8 2.0 copy-start.2
  29.1 2.0 copy-start.2
  34.8 188.4 %all-gather.8.cloned.1.call-start = ((), (), s32[]{:S(2)}) async-start(), calls=%async_computation.2 | async-start | bytes 2129920 | tf_op jit(solution)/shard_map/all_gather | solution.py:97
  144.7 82.6 %copy-start.5 = (bf16[2,256,1,128]{3,1,2,0:T(8,128)(2,1)S(1)}, bf16[2,256,1,128]{3,1,2,0:T(8,128)(2,1)}, u32[]{:S(2)}) copy-start(bf16[2,256,1,128]{3,1,2,0:T(8,128)(2,1)} %param.22) | copy-start | bytes 393220
  144.8 82.6 %copy-start.7 = (bf16[4,2,1,8,128]{4,3,2,1,0:T(8,128)(2,1)S(1)}, bf16[4,2,1,8,128]{4,3,2,1,0:T(8,128)(2,1)}, u32[]{:S(2)}) copy-start(bf16[4,2,1,8,128]{4,3,2,1,0:T(8,128)(2,1)} %param.24) | copy-start | bytes 49156
  144.8 196.5 %copy-start.6 = (bf16[2,256,1,128]{3,1,2,0:T(8,128)(2,1)S(1)}, bf16[2,256,1,128]{3,1,2,0:T(8,128)(2,1)}, u32[]{:S(2)}) copy-start(bf16[2,256,1,128]{3,1,2,0:T(8,128)(2,1)} %param.23) | copy-start | bytes 393220
  227.4 432.7 %copy-start.3 = (bf16[2,128,1,128]{3,1,0,2:T(8,128)(2,1)}, bf16[2,128,1,128]{3,1,0,2:T(8,128)(2,1)S(1)}, u32[]{:S(2)}) copy-start(bf16[2,128,1,128]{3,1,0,2:T(8,128)(2,1)S(1)} %get-tuple-element.105) | copy-start | bytes 196612
  227.4 432.7 %copy-start.4 = (bf16[2,128,1,128]{3,1,0,2:T(8,128)(2,1)}, bf16[2,128,1,128]{3,1,0,2:T(8,128)(2,1)S(1)}, u32[]{:S(2)}) copy-start(bf16[2,128,1,128]{3,1,0,2:T(8,128)(2,1)S(1)} %get-tuple-element.106) | copy-start | bytes 196612
Sparse Core Ops, SparseCore 0:
  16.6 83.3 all-gather.5
  102.0 38.5 all-gather.3
  143.7 79.3 all-gather.7
where the time goes:
time: 667 us
  blocking collectives  432 us (65%)
  waiting for transfers between devices  184 us (28%)
  between operations  14 us (2%)
  matrix products  13.1 us (2%)
  other arithmetic  10.8 us (2%)
  starting transfers between devices  7.38 us (1%)
    psum x1, blocking collectives, body(): lax.psum((weight_sum * rescale, weighted * rescale[..., None]), 'seq')  220 us
    pmax x1, blocking collectives, body(): global_peak = lax.pmax(row_peak, 'seq')  113 us
    psum x1, blocking collectives, body(): summed = lax.psum(partial_value, 'head')  98.6 us
    all_gather x1, waiting for transfers between devices, body(): lax.all_gather(beacon_wv, 'seq', axis=0, tiled=True)  78.4 us
    all_gather x1, waiting for transfers between devices, body(): lax.all_gather(beacon_wk, 'seq', axis=0, tiled=True)  64.2 us
    all_gather x1, waiting for transfers between devices, body(): pooled_whole = lax.all_gather(pooled_flat, 'head', axis=1, tiled=True)  40.7 us
  transfers between devices with their start and end apart: 5, of which 3 were waited for; matrix products, arithmetic and copies ran while one was open for 3% of the time, Pallas kernels for 0%

commit v1 on v0

--- a/solution.py
+++ b/solution.py
@@ -62,6 +62,12 @@
     decode_queries,
     out_weight,
 ):
+
+    def group_the_keys(x_in):
+        y_new = jnp.stack([x_in for _ in range(lax.psum(1, "seq"))])
+        back = lax.all_to_all(y_new, "seq", 0, 0)
+        return jnp.concatenate(back, axis=0)
+
     requests = raw_keys.shape[0]
     kv_local = raw_keys.shape[2]
     head_dim = raw_keys.shape[3]
@@ -92,11 +98,7 @@
         lax.all_gather(beacon_wk, "seq", axis=0, tiled=True),
         preferred_element_type=jnp.float32,
     )
-    value_sum = jnp.dot(
-        pooled_whole,
-        lax.all_gather(beacon_wv, "seq", axis=0, tiled=True),
-        preferred_element_type=jnp.float32,
-    )
+    value_sum = jnp.dot(pooled_whole, group_the_keys(beacon_wv), preferred_element_type=jnp.float32)
     made_keys = key_sum
     made_values = value_sum
     made_keys = made_keys.reshape(requests, NB, kv_local, head_dim)

time: 667 us -> 629 us (0.943)
  waiting for transfers between devices: 184 us -> 130 us
  starting transfers between devices: 7.38 us -> 21.8 us
    all_gather x1 -> x0, waiting for transfers between devices: 78.4 us -> none  [body(): lax.all_gather(beacon_wv, 'seq', axis=0, tiled=True)]
    all_gather x1, waiting for transfers between devices: 64.2 us -> 89.5 us  [body(): lax.all_gather(beacon_wk, 'seq', axis=0, tiled=True)]
    all_to_all x0 -> x1, starting transfers between devices: none -> 14.5 us  [group_the_keys(): back = lax.all_to_all(y_new, 'seq', 0, 0)]
  transfers between devices with their start and end apart: 5 -> 5, of which waited for: 3 -> 2; matrix products, arithmetic and copies ran while one was open for 3% -> 4% of each run, Pallas kernels for 0% -> 0%
where the time goes in v1:
time: 629 us
  blocking collectives  431 us (69%)
  waiting for transfers between devices  130 us (21%)
  starting transfers between devices  21.8 us (3%)
  between operations  14.3 us (2%)
  matrix products  12.4 us (2%)
  other arithmetic  11.6 us (2%)
  local copies, waits for them, and re-layouts  7.48 us (1%)
    psum x1, blocking collectives, body(): lax.psum((weight_sum * rescale, weighted * rescale[..., None]), 'seq')  220 us
    pmax x1, blocking collectives, body(): global_peak = lax.pmax(row_peak, 'seq')  117 us
    psum x1, blocking collectives, body(): summed = lax.psum(partial_value, 'head')  94.2 us
    all_gather x1, waiting for transfers between devices, body(): lax.all_gather(beacon_wk, 'seq', axis=0, tiled=True)  89.5 us
    all_gather x1, waiting for transfers between devices, body(): pooled_whole = lax.all_gather(pooled_flat, 'head', axis=1, tiled=True)  40.7 us
    all_to_all x1, starting transfers between devices, group_the_keys(): back = lax.all_to_all(y_new, 'seq', 0, 0)  14.5 us
  transfers between devices with their start and end apart: 5, of which 2 were waited for; matrix products, arithmetic and copies ran while one was open for 4% of the time, Pallas kernels for 0%

profile of v1, /device:TPU:1, one launch (start us, length us, event | category | flops | bytes accessed | tf_op | source)
XLA Modules:
  0.0 628.6 jit_solution(13770961011729380721)
XLA Ops:
  7.2 0.0 copy-start
  7.2 0.0 copy-start.1
  7.2 0.0 all-gather.5.cloned.1.call-start
  7.2 1.0 slice.9
  8.2 4.7 collective-permute-start.1
  12.9 0.9 slice.8
  13.8 2.6 collective-permute-start
  16.4 0.0 all-gather.5.cloned.1.call-update
  16.4 0.0 all-gather.3.cloned.1.call-start
  16.5 0.7 broadcast_subtract_fusion
  17.2 0.7 iota_add_fusion
  17.9 1.2 copy.32
  19.2 0.7 broadcast_add_fusion
  19.9 0.7 compare_or_fusion
  20.6 1.0 fusion.45
  21.7 0.1 multiply_add_fusion
  21.8 0.0 collective-permute-done
  21.8 1.1 pad_maximum_fusion
  22.9 0.0 collective-permute-done.1
  22.9 1.0 copy.31
  23.9 0.9 pad_maximum_fusion.1
  24.8 0.0 copy-done.1
  24.8 8.6 %while.12 = (s32[]{:T(128)}, f32[2,128,1,8]{1,3,2,0:T(8,128)S(1)}, f32[2,128,1,8,128]{1,4,3,2,0:T(8,128)S(1)}, pred[2,1280]{1,0:T(4,128)(4,1)S(1)}, s32[2,1280]{...) while((s32[]{:T(128)}, f32[2,128,1,8]{1,3,2,0:T(8,128)S(1)}, ...), condition=%wide.region_3.4_spmd, body=%wide.region_0.3_spmd.sunk | while | flops 685837312 | bytes 21023128 | solution.py:48
  24.9 0.9 compare_and_fusion.3
  25.8 0.9 fusion.66
  26.8 0.0 copy-done.2
  26.8 1.2 fusion.68
  27.9 1.1 fusion.67
  29.1 0.0 copy-start.2
  29.2 0.9 compare_and_fusion.3
  30.2 0.9 fusion.66
  31.1 1.2 fusion.68
  32.3 1.1 fusion.67
  33.4 0.0 copy-start.4
  33.4 0.1 divide_convert_fusion
  33.5 0.3 copy.34
  33.8 0.9 copy.60
  34.8 0.0 all-gather.3.cloned.1.call-update
  34.8 0.0 copy-done.4
  34.8 1.9 stack.2
  36.7 14.5 %all-to-all-start = ((bf16[64,128,128]{2,1,0:T(8,128)(2,1)}), bf16[64,128,128]{2,1,0:T(8,128)(2,1)S(1)}, u32[]{:S(2)}, u32[]{:S(2)}) async-start(bf16[64,128,128]{2,1,0:T(8,128)(2,1)} %stack.2), calls=%async_computation | async-start | bytes 4194304 | tf_op jit(solution)/shard_map/all_to_all | solution.py:68
  51.2 0.0 copy-start.5
  51.2 0.0 copy-start.7
  51.2 0.1 iota_compare_fusion.1
  51.3 0.1 iota_compare_fusion
  51.3 0.1 compare_and_fusion.1
  51.4 89.5 %all-gather.5.cloned.1.call-done = bf16[8192,128]{1,0:T(8,128)(2,1)} async-done(((bf16[128,128]{1,0:T(8,128)(2,1)}), bf16[8192,128]{1,0:T(8,128)(2,1)}) %all-gather.5.cloned.1.call-update) | async-done | bytes 2097168 | tf_op jit(solution)/shard_map/all_gather | solution.py:98
  140.9 40.7 %all-gather.3.cloned.1.call-done = bf16[256,8192]{1,0:T(8,128)(2,1)} async-done(((bf16[256,1024]{1,0:T(8,128)(2,1)}), bf16[256,8192]{1,0:T(8,128)(2,1)}) %all-gather.3.cloned.1.call-update) | async-done | bytes 4194320 | tf_op jit(solution)/shard_map/all_gather | solution.py:95
  181.6 4.1 fusion.49
  185.7 0.0 copy-start.6
  185.7 0.1 select_convert_fusion
  185.9 0.3 select_reduce_fusion
  186.2 116.8 %pmax.7 = f32[2,1,4,8]{3,2,0,1:T(4,128)S(1)} all-reduce(f32[2,1,4,8]{3,2,0,1:T(4,128)S(1)} %bitcast.161), channel_id=1, replica_groups=mesh['seq'=64,'head'=8] {'seq'}, use_global_device_ids=true, to_apply=%region_5.6 | all-reduce | flops 64 | bytes 512 | tf_op jit(solution)/shard_map/pmax | solution.py:132
  303.0 0.2 bitcast_reduce_fusion
  303.1 0.7 fusion.55
  303.9 0.0 all-to-all-done
  303.9 3.4 fusion.25
  307.3 0.0 copy-start.3
  307.3 0.2 fusion.26
  307.6 219.7 %all-reduce = (f32[2,1,4,8,128]{4,3,2,0,1:T(8,128)S(1)}, f32[2,4,8]{2,1,0:T(4,128)S(1)}) all-reduce(f32[2,1,4,8,128]{4,3,2,0,1:T(8,128)S(1)} %fusion.26, f32[2,4,8]{2,1,0:T(4,128)S(1)} %get-tuple-element.101), channel_id=1, replica_groups=mesh['seq'=64,'head'=8] {'seq'}, use_global_device_ids=true, to_apply=%region_6.7 | all-reduce | flops 8256 | bytes 66048 | tf_op jit(solution)/shard_map/psum | solution.py:134
  527.3 0.1 fusion.42
  527.4 0.1 fusion.38
  527.6 94.2 %psum.23 = bf16[8,128]{1,0:T(8,128)(2,1)} all-reduce(f32[8,128]{1,0:T(8,128)S(1)} %fusion.38), channel_id=1, replica_groups=mesh['seq'=64,'head'=8] {'head'}, use_global_device_ids=true, to_apply=%region_9.10 | all-reduce | flops 1024 | bytes 6144 | tf_op jit(solution)/shard_map/psum | solution.py:142
  621.8 0.0 copy-done.3
  (24 shorter events, 0.3 us)
Async XLA Ops:
  7.2 520.3 %copy-start = (bf16[1024,128]{1,0:T(8,128)(2,1)S(1)}, bf16[1024,128]{1,0:T(8,128)(2,1)}, u32[]{:S(2)}) copy-start(bf16[1024,128]{1,0:T(8,128)(2,1)} %param.25) | copy-start | bytes 786436
  7.2 17.6 %copy-start.1 = (bf16[2,128,1,8,128]{4,3,2,1,0:T(8,128)(2,1)S(1)}, bf16[2,128,1,8,128]{4,3,2,1,0:T(8,128)(2,1)}, u32[]{:S(2)}) copy-start(bf16[2,128,1,8,128]{4,3,2,1,0:T(8,128)(2,1)} %param.19) | copy-start | bytes 1572868
  7.2 133.7 %all-gather.5.cloned.1.call-start = ((), (), s32[]{:S(2)}) async-start(), calls=%async_computation.2 | async-start | bytes 2129920 | tf_op jit(solution)/shard_map/all_gather | solution.py:98
  8.2 14.6 %collective-permute-start.1 = (bf16[2,256,1,128]{3,1,0,2:T(8,128)(2,1)S(1)}, bf16[2,256,1,128]{3,1,0,2:T(8,128)(2,1)}, u32[]{:S(2)}, u32[]{:S(2)}) collective-permute-start(bf16[2,256,1,128]{3,1,0,2:T(8,128)(2,1)S(1)} %slice.9), channel_id=1, source_target_pairs={{0,8},{8,16},{16,24},{24,32},{32,40},{40,48},{48,56},{56,64},{64,7... | collective-permute-start | bytes 393224 | tf_op jit(solution)/shard_map/ppermute | solution.py:18
  13.8 7.9 %collective-permute-start = (bf16[2,256,1,128]{3,1,0,2:T(8,128)(2,1)S(1)}, bf16[2,256,1,128]{3,1,0,2:T(8,128)(2,1)S(1)}, u32[]{:S(2)}, u32[]{:S(2)}) collective-permute-start(bf16[2,256,1,128]{3,1,0,2:T(8,128)(2,1)S(1)} %slice.8), channel_id=1, source_target_pairs={{0,8},{8,16},{16,24},{24,32},{32,40},{40,48},{48,56},{56,64},{64,7... | collective-permute-start | bytes 393224 | tf_op jit(solution)/shard_map/ppermute | solution.py:18
  16.4 165.2 %all-gather.3.cloned.1.call-start = ((), (), s32[]{:S(2)}) async-start(), calls=%async_computation.1 | async-start | bytes 4718592 | tf_op jit(solution)/shard_map/all_gather | solution.py:95
  24.8 2.0 copy-start.2
  29.1 2.0 copy-start.2
  33.4 1.4 copy-start.4
  36.7 267.2 %all-to-all-start = ((bf16[64,128,128]{2,1,0:T(8,128)(2,1)}), bf16[64,128,128]{2,1,0:T(8,128)(2,1)S(1)}, u32[]{:S(2)}, u32[]{:S(2)}) async-start(bf16[64,128,128]{2,1,0:T(8,128)(2,1)} %stack.2), calls=%async_computation | async-start | bytes 4194304 | tf_op jit(solution)/shard_map/all_to_all | solution.py:68
  51.2 134.7 %copy-start.5 = (bf16[2,256,1,128]{3,1,2,0:T(8,128)(2,1)S(1)}, bf16[2,256,1,128]{3,1,2,0:T(8,128)(2,1)}, u32[]{:S(2)}) copy-start(bf16[2,256,1,128]{3,1,2,0:T(8,128)(2,1)} %param.22) | copy-start | bytes 393220
  51.2 134.7 %copy-start.7 = (bf16[4,2,1,8,128]{4,3,2,1,0:T(8,128)(2,1)S(1)}, bf16[4,2,1,8,128]{4,3,2,1,0:T(8,128)(2,1)}, u32[]{:S(2)}) copy-start(bf16[4,2,1,8,128]{4,3,2,1,0:T(8,128)(2,1)} %param.24) | copy-start | bytes 49156
  185.7 121.6 %copy-start.6 = (bf16[2,256,1,128]{3,1,2,0:T(8,128)(2,1)S(1)}, bf16[2,256,1,128]{3,1,2,0:T(8,128)(2,1)}, u32[]{:S(2)}) copy-start(bf16[2,256,1,128]{3,1,2,0:T(8,128)(2,1)} %param.23) | copy-start | bytes 393220
  307.3 314.5 %copy-start.3 = (bf16[2,128,128]{2,1,0:T(8,128)(2,1)}, bf16[2,128,128]{2,1,0:T(8,128)(2,1)S(1)}, u32[]{:S(2)}) copy-start(bf16[2,128,128]{2,1,0:T(8,128)(2,1)S(1)} %fusion.25) | copy-start | bytes 196612
Sparse Core Ops, SparseCore 0:
  16.6 124.2 all-gather.4
  143.0 38.5 all-gather.2
